TPU v7x, 32 devices: a whole 2x2x4 slice. The times are simulated.
32 devices in a mesh: groups: 2 (over x), orient: 16 (over z, y, core).
Axes of the slice: x: 2, y: 2, z: 4, core: 2. Of those that a mesh axis runs over, the one named last changes fastest.
Arguments:
- images: bfloat16 [8192, 16384], P(('groups', 'orient')), parts along dimension 0, may hold values from -6 to 6
- projections: bfloat16 [32, 16384], P(('groups', 'orient')), parts along dimension 0, may hold values from -0.046875 to 0.046875
- noise_weight: float32 [32768], P('groups'), parts along dimension 0, may hold values from 0.3 to 3
- lognorm: float32 [8192], P(('groups', 'orient')), parts along dimension 0, may hold values from 4 to 6
- eligible: int32 [8192, 16], P(('groups', 'orient')), parts along dimension 0, may hold values 0 or 1
Outputs:
- orient_sums: float32 [32, 16384], P(('groups', 'orient')), parts along dimension 0
There are 2 independent parts, one for each index of `groups`. A program takes and returns all parts, laid end to end along the dimension named above; each array names one. Nothing has to cross between parts.
All inputs are finite; a program needn't handle non-finite values. No bound on the sum of `eligible` on one device may be relied on, other than what follows from the above.
Results may differ from a plain program's by a relative error of at most 0.0044.
Values may be sent and summed in bfloat16 or wider, within the bound.
A program may use at most 64 MiB of HBM per device.

v0:
```python
import jax
import jax.numpy as jnp
from jax import lax
from jax.sharding import PartitionSpec as P


def body(images, projections, noise_weight, lognorm, eligible):
    ori_dev = projections.shape[0]
    mask_rows = jnp.repeat(eligible, ori_dev, axis=1).astype(jnp.float32)
    piece = lax.all_gather(projections, "orient", axis=0, tiled=True)
    piece_float = piece.astype(jnp.float32)
    power = jnp.sum(piece_float * piece_float * noise_weight[None, :], axis=1)
    raw = lax.dot_general(
        images, piece, (((1,), (1,)), ((), ())), preferred_element_type=jnp.float32
    )
    weights = (mask_rows * jnp.exp(raw - 0.5 * power[None, :] - lognorm[:, None])).astype(
        jnp.bfloat16
    )
    term = lax.dot_general(
        weights, images, (((0,), (0,)), ((), ())), preferred_element_type=jnp.float32
    )
    result = lax.psum_scatter(term, "orient", scatter_dimension=0, tiled=True)
    return result


def solution(mesh):
    in_specs = (
        P(("groups", "orient"), None),
        P(("groups", "orient"), None),
        P("groups"),
        P(("groups", "orient")),
        P(("groups", "orient"), None),
    )
    out_specs = P(("groups", "orient"), None)
    return jax.shard_map(body, mesh=mesh, in_specs=in_specs, out_specs=out_specs, check_vma=False)
```

profile of v0, /device:TPU:0, one launch (start us, length us, event | category | flops | bytes accessed | tf_op | source)
XLA Modules:
  0.0 146.7 jit_solution(10150825099016115037)
XLA Ops:
  6.5 0.0 all-reduce.3.cloned.1.call-start
  6.5 26.3 %all-gather = bf16[16,1,16384]{2,1,0:T(2,128)(2,1)S(1)} all-gather(bf16[1,1,16384]{2,1,0:T(2,128)(2,1)} %bitcast.9), channel_id=1, replica_groups=mesh['groups'=2,'orient'=16] {'orient'}, dimensions={0}, use_global_device_ids=true | all-gather | bytes 557056 | tf_op jit(solution)/shard_map/all_gather | solution.py:10
  32.9 1.5 %multiply_reduce_fusion = f32[16]{0:T(128)S(1)} fusion(f32[16384]{0:T(1024)} %param.7, bf16[16,1,16384]{2,1,0:T(2,128)(2,1)S(1)} %all-gather), kind=kLoop, calls=%fused_computation.5 | loop fusion | flops 1048560 | bytes 589888 | tf_op jit(solution)/shard_map/reduce_sum | solution.py:12
  34.4 0.0 copy-start
  34.4 12.5 %fusion.4 = f32[16,16384]{1,0:T(8,128)} fusion(bf16[256,16384]{1,0:T(8,128)(2,1)} %param.5, bf16[16,1,16384]{2,1,0:T(2,128)(2,1)S(1)} %all-gather, s32[256,16]{0,1:T(8,128)} %param.9, f32[256]{0:T(256)} %param.8, f32[16]{0:T(128)S(1)} %broadcast_multiply_fusion), kind=kOutput, calls=%fused_computation.6 | convolution fusion | flops 268455936 | bytes 9978944 | tf_op jit(solution)/shard_map/dot_general | solution.py:19
  46.9 0.0 all-reduce.3.cloned.1.call-update
  46.9 0.0 copy-done
  46.9 0.6 dynamic-slice
  47.5 90.0 %all-reduce.3.cloned.1.call-done = f32[16,16384]{1,0:T(8,128)} async-done(((f32[16,16384]{1,0:T(8,128)}), f32[16,16384]{1,0:T(8,128)}) %all-reduce.3.cloned.1.call-update) | async-done | bytes 1048592
  137.5 2.3 %constant_dynamic-slice_fusion = f32[1,16384]{1,0:T(1,128)} fusion(f32[16,16384]{1,0:T(8,128)} %all-reduce.3.cloned.1.call-done, u32[]{:T(128)} %bitcast.1), kind=kLoop, calls=%fused_computation.12 | loop fusion | bytes 131076
  (1 shorter events, 0.0 us)
Async XLA Ops:
  6.5 131.0 %all-reduce.3.cloned.1.call-start = ((), (), s32[]{:S(2)}) async-start(), calls=%async_computation | async-start | bytes 2097152
  34.4 12.5 %copy-start = (u32[32]{0:T(128)S(1)}, u32[32]{0:T(128)}, u32[]{:S(2)}) copy-start(u32[32]{0:T(128)} %constant.7) | copy-start | bytes 388
Sparse Core Ops, SparseCore 0:
  47.0 90.4 all-reduce.2
where the time goes:
time: 147 us
  waiting for transfers between devices  90 us (61%)
  blocking collectives  26.3 us (18%)
  between operations  13.4 us (9%)
  matrix products  12.5 us (9%)
  local copies, waits for them, and re-layouts  2.93 us (2%)
  other arithmetic  1.54 us (1%)
    unnamed x2, waiting for transfers between devices  90 us
    all_gather x1, blocking collectives, body(): piece = lax.all_gather(projections, 'orient', axis=0, tiled=True)  26.3 us
    dot_general x1, matrix products, body(): lax.dot_general(weights, images, (((0,), (0,)), ((), ())), preferred_elem...  12.5 us
  transfers between devices with their start and end apart: 1, of which 1 were waited for; matrix products, arithmetic and copies ran while one was open for 0% of the time, Pallas kernels for 0%

commit v1 on v0

v1 whole, which is shorter than its diff:
```python
import functools

import jax
import jax.numpy as jnp
from jax import lax
from jax.experimental import pallas as pl
from jax.experimental.pallas import tpu as pltpu
from jax.sharding import PartitionSpec as P

MESH = pl.DeviceIdType.MESH
LANES = 128


def kernel(
    outer, inner, gq, rq, iq,
    proj_ref, noise_ref, lognorm_ref, eligible_ref, images_hbm, out_ref,
    images, gathered, staged, term, core_out, core_in, inner_out, inner_in, inner_own,
    outer_out, outer_in,
    img_sem, g_send, g_recv, c_send, c_recv, i_send, i_recv, o_send, o_recv,
):
    n = outer * inner * 2
    tiles = proj_ref.shape[0]
    feats = tiles * LANES
    me = lax.axis_index("orient")
    c = me % 2
    b = (me // 2) % inner
    a = me // (2 * inner)
    sib = 1 - c

    def at(a_, b_, c_):
        return {"orient": (a_ * inner + b_) * 2 + c_}

    def slot(a_, b_, c_):
        return (c_ * inner + b_) * outer + a_

    a_others = [(a + k) % outer for k in range(1, outer)]
    b_others = [(b + k) % inner for k in range(1, inner)]

    width = feats // iq
    loads = []
    for q in range(iq):
        part = pl.ds(q * width, width)
        loads.append(pltpu.make_async_copy(images_hbm.at[:, part], images.at[:, part], img_sem.at[q]))
        loads[-1].start()

    barrier = pltpu.get_barrier_semaphore()
    peers = [at(a_, b, c) for a_ in a_others] + [at(a, b_, c) for b_ in b_others] + [at(a, b, sib)]
    for peer in peers:
        pl.semaphore_signal(barrier, inc=1, device_id=peer, device_id_type=MESH)
    pl.semaphore_wait(barrier, len(peers))

    sends = []
    grow = tiles // gq

    def push(q, row, src, to):
        rows = pl.ds(q * grow, grow)
        copy = pltpu.make_async_remote_copy(
            src_ref=src.at[rows], dst_ref=gathered.at[row, rows],
            send_sem=g_send.at[len(sends)], recv_sem=g_recv.at[q, row],
            device_id=to, device_id_type=MESH,
        )
        copy.start()
        sends.append(copy)

    def arrived(q, row):
        rows = pl.ds(q * grow, grow)
        pltpu.make_async_remote_copy(
            src_ref=gathered.at[row, rows], dst_ref=gathered.at[row, rows],
            send_sem=g_send.at[0], recv_sem=g_recv.at[q, row],
            device_id=at(a, b, sib), device_id_type=MESH,
        ).wait_recv()

    mine = slot(a, b, c)
    for q in range(gq):
        for a_ in a_others:
            push(q, mine, proj_ref, at(a_, b, c))
        for b_ in b_others:
            push(q, mine, proj_ref, at(a, b_, c))
        push(q, mine, proj_ref, at(a, b, sib))
    gathered[mine] = proj_ref[...]

    s_at = lax.broadcasted_iota(jnp.int32, (n, n), 0)
    j_at = lax.broadcasted_iota(jnp.int32, (n, n), 1)
    s_a = s_at & (outer - 1)
    s_b = lax.shift_right_logical(s_at, outer.bit_length() - 1) & (inner - 1)
    s_c = lax.shift_right_logical(s_at, (outer * inner).bit_length() - 1)
    order = ((s_a * inner + s_b) * 2 + s_c == j_at).astype(jnp.float32).astype(jnp.bfloat16)
    mask = lax.dot_general(
        order, eligible_ref[...].astype(jnp.float32).astype(jnp.bfloat16),
        (((1,), (1,)), ((), ())), preferred_element_type=jnp.float32,
    )

    for q in range(gq):
        for a_ in a_others:
            row = slot(a_, b, c)
            arrived(q, row)
            for b_ in b_others:
                push(q, row, gathered.at[row], at(a, b_, c))
            push(q, row, gathered.at[row], at(a, b, sib))
        for b_ in b_others:
            for a_ in [a] + a_others:
                row = slot(a_, b_, c)
                arrived(q, row)
                push(q, row, gathered.at[row], at(a, b, sib))

    step = 8
    raw = jnp.zeros((n, images.shape[0]), jnp.float32)
    power = jnp.zeros((n, LANES), jnp.float32)
    for q in range(gq):
        for a_ in [a] + a_others:
            for b_ in [b] + b_others:
                arrived(q, slot(a_, b_, sib))
        for i in range(iq * q // gq, iq * (q + 1) // gq):
            loads[i].wait()

        def widen(s, carry, q=q):
            staged[pl.ds(pl.multiple_of(s * tiles + q * grow, 8), grow), :] = gathered[
                s, pl.ds(q * grow, grow), :
            ].astype(jnp.float32)
            return carry

        lax.fori_loop(0, n, widen, 0)

        def score(p, carry, q=q):
            raw, power = carry
            first = q * grow + p * step
            pieces = []
            for r in range(step):
                x = staged[pl.ds(first + r, n, stride=tiles), :]
                power = power + x * x * noise_ref[pl.ds(first + r, 1), :]
                pieces.append(x.astype(jnp.bfloat16))
            piece = jnp.concatenate(pieces, axis=1)
            cols = pl.ds(pl.multiple_of(first * LANES, step * LANES), step * LANES)
            raw = raw + lax.dot_general(
                piece, images[:, cols], (((1,), (1,)), ((), ())), preferred_element_type=jnp.float32
            )
            return raw, power

        raw, power = lax.fori_loop(0, grow // step, score, (raw, power))

    scores = raw - 0.5 * jnp.sum(power, axis=1, keepdims=True)
    weights = (mask * jnp.exp(scores - lognorm_ref[...])).astype(jnp.bfloat16)

    rrow = tiles // rq
    half = n // 2

    def copy_of(src, dst, send, recv, to):
        return pltpu.make_async_remote_copy(
            src_ref=src, dst_ref=dst, send_sem=send, recv_sem=recv, device_id=to, device_id_type=MESH
        )

    def summed(s, q):
        return term[pl.ds(q * rrow * n + s, rrow, stride=n), :]

    def compute(q):
        def piece(p, carry):
            first = q * rrow + p * step
            cols = pl.ds(pl.multiple_of(first * LANES, step * LANES), step * LANES)
            t = jnp.dot(weights, images[:, cols], preferred_element_type=jnp.float32)
            for r in range(step):
                term[pl.ds(pl.multiple_of((first + r) * n, 8), n), :] = t[:, r * LANES:(r + 1) * LANES]
            return carry

        lax.fori_loop(0, rrow // step, piece, 0)
        rows = pl.ds(q * rrow, rrow)

        def pack(h, carry):
            core_out[h, rows, :] = summed(sib * half + h, q).astype(jnp.bfloat16)
            return carry

        lax.fori_loop(0, half, pack, 0)
        copy = copy_of(core_out.at[:, rows], core_in.at[:, rows], c_send.at[q], c_recv.at[q], at(a, b, sib))
        copy.start()
        return copy

    def after_core(q, copy):
        copy.wait_recv()
        rows = pl.ds(q * rrow, rrow)
        copies = []
        for k, b_ in enumerate(b_others):
            def pack(a_, carry, b_=b_):
                h = b_ * outer + a_
                value = summed(c * half + h, q) + core_in[h, rows, :].astype(jnp.float32)
                inner_out[b_, a_, rows, :] = value.astype(jnp.bfloat16)
                return carry

            lax.fori_loop(0, outer, pack, 0)
            copies.append(copy_of(
                inner_out.at[b_, :, rows], inner_in.at[k, :, rows], i_send.at[q, k], i_recv.at[q, k], at(a, b_, c)
            ))
            copies[-1].start()

        def keep(a_, carry):
            h = b * outer + a_
            inner_own[a_, rows, :] = summed(c * half + h, q) + core_in[h, rows, :].astype(jnp.float32)
            return carry

        lax.fori_loop(0, outer, keep, 0)
        return copies

    def after_inner(q, copies):
        for copy in copies:
            copy.wait_recv()
        rows = pl.ds(q * rrow, rrow)

        def total(a_):
            value = inner_own[a_, rows, :]
            for k in range(inner - 1):
                value = value + inner_in[k, a_, rows, :].astype(jnp.float32)
            return value

        done = []
        for k, a_ in enumerate(a_others):
            outer_out[k, rows, :] = total(a_).astype(jnp.bfloat16)
            done.append(copy_of(
                outer_out.at[k, rows], outer_in.at[k, rows], o_send.at[q, k], o_recv.at[q, k], at(a_, b, c)
            ))
            done[-1].start()
        out_ref[rows, :] = total(a)
        return done

    def after_outer(q, copies):
        rows = pl.ds(q * rrow, rrow)
        value = out_ref[rows, :]
        for k, copy in enumerate(copies):
            copy.wait_recv()
            value = value + outer_in[k, rows, :].astype(jnp.float32)
        out_ref[rows, :] = value

    core_copies, inner_copies, outer_copies = {}, {}, {}
    for t in range(rq + 2):
        if t < rq:
            core_copies[t] = compute(t)
        if 0 <= t - 1 < rq:
            inner_copies[t - 1] = after_core(t - 1, core_copies[t - 1])
        if 0 <= t - 2 < rq:
            outer_copies[t - 2] = after_inner(t - 2, inner_copies[t - 2])
    for q in range(rq):
        after_outer(q, outer_copies[q])

    for copy in sends:
        copy.wait_send()
    for q in range(rq):
        for copy in [core_copies[q]] + inner_copies[q] + outer_copies[q]:
            copy.wait_send()


def body(n, images, projections, noise_weight, lognorm, eligible):
    count, feats = images.shape
    tiles = feats // LANES
    chips = n // 2
    inner = 2 ** ((chips.bit_length() - 1) // 2)
    outer = chips // inner
    gq, rq, iq = 2, 4, 4
    half = n // 2
    copies = gq * (n - 1)
    vmem = pl.BlockSpec(memory_space=pltpu.VMEM)
    dma = pltpu.SemaphoreType.DMA
    out = pl.pallas_call(
        functools.partial(kernel, outer, inner, gq, rq, iq),
        out_shape=jax.ShapeDtypeStruct((tiles, LANES), jnp.float32),
        in_specs=[vmem, vmem, vmem, vmem, pl.BlockSpec(memory_space=pl.ANY)],
        out_specs=vmem,
        scratch_shapes=[
            pltpu.VMEM((count, feats), jnp.bfloat16),
            pltpu.VMEM((n, tiles, LANES), jnp.bfloat16),
            pltpu.VMEM((n * tiles, LANES), jnp.float32),
            pltpu.VMEM((n * tiles, LANES), jnp.float32),
            pltpu.VMEM((half, tiles, LANES), jnp.bfloat16),
            pltpu.VMEM((half, tiles, LANES), jnp.bfloat16),
            pltpu.VMEM((inner, outer, tiles, LANES), jnp.bfloat16),
            pltpu.VMEM((inner - 1, outer, tiles, LANES), jnp.bfloat16),
            pltpu.VMEM((outer, tiles, LANES), jnp.float32),
            pltpu.VMEM((outer - 1, tiles, LANES), jnp.bfloat16),
            pltpu.VMEM((outer - 1, tiles, LANES), jnp.bfloat16),
            dma((iq,)),
            dma((copies,)), dma((gq, n)),
            dma((rq,)), dma((rq,)),
            dma((rq, inner - 1)), dma((rq, inner - 1)),
            dma((rq, outer - 1)), dma((rq, outer - 1)),
        ],
        compiler_params=pltpu.CompilerParams(
            collective_id=0, has_side_effects=True, vmem_limit_bytes=56 * 1024 * 1024
        ),
    )(
        projections.reshape(tiles, LANES), noise_weight.reshape(tiles, LANES),
        lognorm.reshape(1, count), eligible, images,
    )
    return out.reshape(1, feats)


def solution(mesh):
    in_specs = (
        P(("groups", "orient"), None),
        P(("groups", "orient"), None),
        P("groups"),
        P(("groups", "orient")),
        P(("groups", "orient"), None),
    )
    out_specs = P(("groups", "orient"), None)
    return jax.shard_map(
        functools.partial(body, mesh.shape["orient"]),
        mesh=mesh, in_specs=in_specs, out_specs=out_specs, check_vma=False,
    )
```

time: 147 us -> 40.1 us (0.27)
  waiting for transfers between devices: 90 us -> 0 us
  Pallas kernels: 0 us -> 35.2 us
  blocking collectives: 26.3 us -> 0 us
  between operations: 13.4 us -> 0.01 us
  matrix products: 12.5 us -> 0 us
    unnamed x2 -> x0, waiting for transfers between devices: 90 us -> none
    pallas_call x0 -> x1, Pallas kernels: none -> 35.2 us  [body(): pl.pallas_call(functools.partial(kernel, outer, inner, gq, rq, iq), out_s...]
    all_gather x1 -> x0, blocking collectives: 26.3 us -> none  [body(): piece = lax.all_gather(projections, 'orient', axis=0, tiled=True)]
    dot_general x1 -> x0, matrix products: 12.5 us -> none  [body(): lax.dot_general(weights, images, (((0,), (0,)), ((), ())), preferred_elem...]
    unnamed x0 -> x1, other arithmetic: none -> 1.63 us
    reduce_sum x1 -> x0, other arithmetic: 1.53 us -> none  [body(): power = jnp.sum(piece_float * piece_float * noise_weight[None, :], axis=1)]
  transfers between devices with their start and end apart: 1 -> 0, of which waited for: 1 -> 0; matrix products, arithmetic and copies ran while one was open for 0% -> 0% of each run, Pallas kernels for 0% -> 0%
where the time goes in v1:
time: 40.1 us; the launch traced here: 39.8 us
  Pallas kernels  35.2 us (88%)
  local copies, waits for them, and re-layouts  2.93 us (7%)
  other arithmetic  1.63 us (4%)
    pallas_call x1, Pallas kernels, body(): pl.pallas_call(functools.partial(kernel, outer, inner, gq, rq, iq), out_s...  35.2 us
    unnamed x2, local copies, waits for them, and re-layouts  2.93 us
    unnamed x1, other arithmetic  1.63 us

profile of v1, /device:TPU:0, one launch (start us, length us, event | category | flops | bytes accessed | tf_op | source)
XLA Modules:
  0.0 39.8 jit_solution(9086524167437357189)
XLA Ops:
  0.0 1.6 %reduce = bf16[16384]{0:T(1024)(128)(2,1)} reduce(bf16[1,16384]{1,0:T(2,128)(2,1)} %param.6, bf16[]{:T(256)} %constant.1), dimensions={0}, to_apply=%param.6.reduce_sub_computation | reduce | bytes 65538 | tf_op args[1]
  1.6 1.5 %copy.6.eligible_ref = s32[256,16]{1,0:T(8,128)} copy(s32[256,16]{0,1:T(8,128)} %param.9) | data formatting | bytes 32768 | tf_op args[4]
  3.1 35.2 %shard_map.55 = f32[128,128]{1,0:T(8,128)} custom-call(bf16[128,128]{1,0:T(8,128)(2,1)} %bitcast.5, f32[128,128]{1,0:T(8,128)} %bitcast.6, f32[1,256]{1,0:T(1,128)} %bitcast.7, s32[256,16]{1,0:T(8,128)} %copy.6.eligible_ref, bf16[256,16384]{1,0:T(8,128)(2,1)} %images_hbm.1), custom_call_target="tpu_custom_call" | custom-call | tf_op jit(solution)/shard_map/pallas_call | solution.py:259
  38.3 1.5 %copy.8 = f32[1,16384]{1,0:T(1,128)} copy(f32[1,16384]{1,0:T(1,128)} %bitcast.4) | data formatting | bytes 131072

commit v2 on v1

v2 whole, which is shorter than its diff:
```python
import functools

import jax
import jax.numpy as jnp
from jax import lax
from jax.experimental import pallas as pl
from jax.experimental.pallas import tpu as pltpu
from jax.sharding import PartitionSpec as P

MESH = pl.DeviceIdType.MESH
LANES = 128


def kernel(
    chips, gq, rq, iq, step,
    row_ref, noise_ref, lognorm_ref, eligible_ref, images_hbm, out_ref,
    images, own_row, gathered, staged, term, core_out, core_in, chip_out, chip_in,
    img_sem, g_send, g_recv, c_send, c_recv, o_send, o_recv,
):
    n = chips * 2
    tiles = noise_ref.shape[0]
    feats = tiles * LANES
    me = lax.axis_index("orient")
    c = me % 2
    a = me // 2
    sib = 1 - c

    def at(a_, c_):
        return {"orient": a_ * 2 + c_}

    def slot(a_, c_):
        return c_ * chips + a_

    others = [(a + k) % chips for k in range(1, chips)]

    width = feats // iq
    loads = []
    for q in range(iq):
        part = pl.ds(q * width, width)
        loads.append(pltpu.make_async_copy(images_hbm.at[:, part], images.at[:, part], img_sem.at[q]))
        loads[-1].start()

    barrier = pltpu.get_barrier_semaphore()
    for peer in [at(a_, c) for a_ in others] + [at(a, sib)]:
        pl.semaphore_signal(barrier, inc=1, device_id=peer, device_id_type=MESH)

    mine = slot(a, c)
    base = pl.multiple_of(mine * tiles, 8)
    wide = row_ref[...].astype(jnp.float32)
    for r in range(tiles):
        staged[pl.ds(base + r, 1), :] = wide[:, r * LANES:(r + 1) * LANES]
    own_row[...] = staged[pl.ds(base, tiles), :].astype(jnp.bfloat16)

    pl.semaphore_wait(barrier, chips)

    sends = []
    grow = tiles // gq

    def push(q, row, src, to):
        rows = pl.ds(q * grow, grow)
        copy = pltpu.make_async_remote_copy(
            src_ref=src.at[rows], dst_ref=gathered.at[row, rows],
            send_sem=g_send.at[len(sends)], recv_sem=g_recv.at[q, row],
            device_id=to, device_id_type=MESH,
        )
        copy.start()
        sends.append(copy)

    def arrived(q, row):
        rows = pl.ds(q * grow, grow)
        pltpu.make_async_remote_copy(
            src_ref=gathered.at[row, rows], dst_ref=gathered.at[row, rows],
            send_sem=g_send.at[0], recv_sem=g_recv.at[q, row],
            device_id=at(a, sib), device_id_type=MESH,
        ).wait_recv()

    def widen(q, row):
        staged[pl.ds(pl.multiple_of(row * tiles + q * grow, 8), grow), :] = gathered[
            row, pl.ds(q * grow, grow), :
        ].astype(jnp.float32)

    for q in range(gq):
        for a_ in others:
            push(q, mine, own_row, at(a_, c))
        push(q, mine, own_row, at(a, sib))

    s_at = lax.broadcasted_iota(jnp.int32, (n, n), 0)
    j_at = lax.broadcasted_iota(jnp.int32, (n, n), 1)
    second = s_at >= chips
    own = jnp.where(second, (s_at - chips) * 2 + 1, s_at * 2)
    order = (own == j_at).astype(jnp.float32).astype(jnp.bfloat16)
    mask = jnp.dot(
        order, eligible_ref[...].astype(jnp.float32).astype(jnp.bfloat16),
        preferred_element_type=jnp.float32,
    )

    for q in range(gq):
        for a_ in others:
            row = slot(a_, c)
            arrived(q, row)
            push(q, row, gathered.at[row], at(a, sib))
            widen(q, row)

    raw = jnp.zeros((n, images.shape[0]), jnp.float32)
    power = jnp.zeros((n, LANES), jnp.float32)
    gstep = min(step, grow)
    for q in range(gq):
        for a_ in [a] + others:
            row = slot(a_, sib)
            arrived(q, row)
            widen(q, row)
        for i in range(iq * q // gq, iq * (q + 1) // gq):
            loads[i].wait()

        def score(p, carry, q=q):
            raw, power = carry
            first = q * grow + p * gstep
            pieces = []
            for r in range(gstep):
                x = staged[pl.ds(first + r, n, stride=tiles), :]
                power = power + x * x * noise_ref[pl.ds(first + r, 1), :]
                pieces.append(x.astype(jnp.bfloat16))
            piece = jnp.concatenate(pieces, axis=1)
            cols = pl.ds(pl.multiple_of(first * LANES, gstep * LANES), gstep * LANES)
            raw = raw + lax.dot_general(
                piece, images[:, cols], (((1,), (1,)), ((), ())), preferred_element_type=jnp.float32
            )
            return raw, power

        raw, power = lax.fori_loop(0, grow // gstep, score, (raw, power))

    scores = raw - 0.5 * jnp.sum(power, axis=1, keepdims=True)
    weights = (mask * jnp.exp(scores - lognorm_ref[...])).astype(jnp.bfloat16)

    rrow = tiles // rq
    rstep = min(step, rrow)

    def copy_of(src, dst, send, recv, to):
        return pltpu.make_async_remote_copy(
            src_ref=src, dst_ref=dst, send_sem=send, recv_sem=recv, device_id=to, device_id_type=MESH
        )

    def summed(s, q):
        return term[pl.ds(q * rrow * n + s, rrow, stride=n), :]

    def compute(q):
        def piece(p, carry):
            first = q * rrow + p * rstep
            cols = pl.ds(pl.multiple_of(first * LANES, rstep * LANES), rstep * LANES)
            t = jnp.dot(weights, images[:, cols], preferred_element_type=jnp.float32)
            for r in range(rstep):
                term[pl.ds(pl.multiple_of((first + r) * n, 8), n), :] = t[:, r * LANES:(r + 1) * LANES]
            return carry

        lax.fori_loop(0, rrow // rstep, piece, 0)
        rows = pl.ds(q * rrow, rrow)

        def pack(h, carry):
            core_out[h, rows, :] = summed(sib * chips + h, q).astype(jnp.bfloat16)
            return carry

        lax.fori_loop(0, chips, pack, 0, unroll=8)
        copy = copy_of(core_out.at[:, rows], core_in.at[:, rows], c_send.at[q], c_recv.at[q], at(a, sib))
        copy.start()
        return copy

    def after_core(q, copy):
        copy.wait_recv()
        rows = pl.ds(q * rrow, rrow)

        def total(a_):
            return summed(c * chips + a_, q) + core_in[a_, rows, :].astype(jnp.float32)

        copies = []
        for k, a_ in enumerate(others):
            chip_out[k, rows, :] = total(a_).astype(jnp.bfloat16)
            copies.append(copy_of(
                chip_out.at[k, rows], chip_in.at[k, rows], o_send.at[q, k], o_recv.at[q, k], at(a_, c)
            ))
            copies[-1].start()
        out_ref[rows, :] = total(a)
        return copies

    def after_chips(q, copies):
        rows = pl.ds(q * rrow, rrow)
        value = out_ref[rows, :]
        for k, copy in enumerate(copies):
            copy.wait_recv()
            value = value + chip_in[k, rows, :].astype(jnp.float32)
        out_ref[rows, :] = value

    core_copies, chip_copies = {}, {}
    for t in range(rq + 1):
        if t < rq:
            core_copies[t] = compute(t)
        if t > 0:
            chip_copies[t - 1] = after_core(t - 1, core_copies[t - 1])
    for q in range(rq):
        after_chips(q, chip_copies[q])

    for copy in sends:
        copy.wait_send()
    for q in range(rq):
        for copy in [core_copies[q]] + chip_copies[q]:
            copy.wait_send()


def body(n, images, projections, noise_weight, lognorm, eligible):
    count, feats = images.shape
    tiles = feats // LANES
    chips = n // 2
    gq, rq, iq, step = 1, 2, 4, 32
    copies = gq * (n - 1)
    vmem = pl.BlockSpec(memory_space=pltpu.VMEM)
    dma = pltpu.SemaphoreType.DMA
    out = pl.pallas_call(
        functools.partial(kernel, chips, gq, rq, iq, step),
        out_shape=pltpu.VMEM((tiles, LANES), jnp.float32),
        in_specs=[vmem, vmem, vmem, vmem, pl.BlockSpec(memory_space=pl.ANY)],
        out_specs=vmem,
        scratch_shapes=[
            pltpu.VMEM((count, feats), jnp.bfloat16),
            pltpu.VMEM((tiles, LANES), jnp.bfloat16),
            pltpu.VMEM((n, tiles, LANES), jnp.bfloat16),
            pltpu.VMEM((n * tiles, LANES), jnp.float32),
            pltpu.VMEM((n * tiles, LANES), jnp.float32),
            pltpu.VMEM((chips, tiles, LANES), jnp.bfloat16),
            pltpu.VMEM((chips, tiles, LANES), jnp.bfloat16),
            pltpu.VMEM((chips - 1, tiles, LANES), jnp.bfloat16),
            pltpu.VMEM((chips - 1, tiles, LANES), jnp.bfloat16),
            dma((iq,)),
            dma((copies,)), dma((gq, n)),
            dma((rq,)), dma((rq,)),
            dma((rq, chips - 1)), dma((rq, chips - 1)),
        ],
        compiler_params=pltpu.CompilerParams(
            collective_id=0, has_side_effects=True, vmem_limit_bytes=56 * 1024 * 1024
        ),
    )(
        projections, noise_weight.reshape(tiles, LANES),
        lognorm.reshape(1, count), eligible.T, images,
    )
    return out.reshape(1, feats)


def solution(mesh):
    in_specs = (
        P(("groups", "orient"), None),
        P(("groups", "orient"), None),
        P("groups"),
        P(("groups", "orient")),
        P(("groups", "orient"), None),
    )
    out_specs = P(("groups", "orient"), None)
    return jax.shard_map(
        functools.partial(body, mesh.shape["orient"]),
        mesh=mesh, in_specs=in_specs, out_specs=out_specs, check_vma=False,
    )
```

time: 40.1 us -> 27.9 us (0.70)
  Pallas kernels: 35.2 us -> 27.1 us
  local copies, waits for them, and re-layouts: 2.93 us -> 0.63 us
  other arithmetic: 1.63 us -> 0 us
    pallas_call x1, Pallas kernels: 35.2 us -> 27.1 us  [body(): pl.pallas_call(functools.partial(kernel, chips, gq, rq, iq, step), out_sh...]
    unnamed x2 -> x1, local copies, waits for them, and re-layouts: 2.93 us -> 0.63 us
    unnamed x1 -> x0, other arithmetic: 1.63 us -> none
where the time goes in v2:
time: 27.9 us; the launch traced here: 27.8 us
  Pallas kernels  27.1 us (97%)
  local copies, waits for them, and re-layouts  0.63 us (2%)
    pallas_call x1, Pallas kernels, body(): pl.pallas_call(functools.partial(kernel, chips, gq, rq, iq, step), out_sh...  27.1 us
    unnamed x1, local copies, waits for them, and re-layouts  0.63 us

profile of v2, /device:TPU:0, one launch (start us, length us, event | category | flops | bytes accessed | tf_op | source)
XLA Modules:
  0.0 27.8 jit_solution(7705477625107114445)
XLA Ops:
  0.0 27.1 %shard_map.55 = f32[128,128]{1,0:T(8,128)S(1)} custom-call(bf16[1,16384]{1,0:T(2,128)(2,1)} %row_ref.1, f32[128,128]{1,0:T(8,128)} %bitcast.5, f32[1,256]{1,0:T(1,128)} %bitcast.7, s32[16,256]{1,0:T(8,128)} %bitcast.6, bf16[256,16384]{1,0:T(8,128)(2,1)} %images_hbm.1), custom_call_target="tpu_custom_call" | custom-call | tf_op jit(solution)/shard_map/pallas_call | solution.py:216
  27.1 0.6 %copy.7 = f32[1,16384]{1,0:T(1,128)} copy(f32[1,16384]{1,0:T(1,128)S(1)} %bitcast.4) | data formatting | bytes 131072

commit v3 on v2

--- a/solution.py
+++ b/solution.py
@@ -209,7 +209,7 @@
     count, feats = images.shape
     tiles = feats // LANES
     chips = n // 2
-    gq, rq, iq, step = 1, 2, 4, 32
+    gq, rq, iq, step = 2, 4, 4, 32
     copies = gq * (n - 1)
     vmem = pl.BlockSpec(memory_space=pltpu.VMEM)
     dma = pltpu.SemaphoreType.DMA

time: 27.9 us -> 27.5 us (0.986)
  Pallas kernels: 27.1 us -> 26.7 us
    pallas_call x1, Pallas kernels: 27.1 us -> 26.7 us  [body(): pl.pallas_call(functools.partial(kernel, chips, gq, rq, iq, step), out_sh...]
where the time goes in v3:
time: 27.5 us; the launch traced here: 27.3 us
  Pallas kernels  26.7 us (97%)
  local copies, waits for them, and re-layouts  0.63 us (2%)
    pallas_call x1, Pallas kernels, body(): pl.pallas_call(functools.partial(kernel, chips, gq, rq, iq, step), out_sh...  26.7 us
    unnamed x1, local copies, waits for them, and re-layouts  0.63 us

profile of v3, /device:TPU:0, one launch (start us, length us, event | category | flops | bytes accessed | tf_op | source)
XLA Modules:
  0.0 27.3 jit_solution(4950554704123182586)
XLA Ops:
  0.0 26.7 %shard_map.55 = f32[128,128]{1,0:T(8,128)S(1)} custom-call(bf16[1,16384]{1,0:T(2,128)(2,1)} %row_ref.1, f32[128,128]{1,0:T(8,128)} %bitcast.5, f32[1,256]{1,0:T(1,128)} %bitcast.7, s32[16,256]{1,0:T(8,128)} %bitcast.6, bf16[256,16384]{1,0:T(8,128)(2,1)} %images_hbm.1), custom_call_target="tpu_custom_call" | custom-call | tf_op jit(solution)/shard_map/pallas_call | solution.py:216
  26.7 0.6 %copy.7 = f32[1,16384]{1,0:T(1,128)} copy(f32[1,16384]{1,0:T(1,128)S(1)} %bitcast.4) | data formatting | bytes 131072
